TPU v7x, 32 devices: a whole 2x2x4 slice. The times are simulated.
32 devices in a mesh: context: 8 (over z, y), tensor: 4 (over x, core).
Axes of the slice: x: 2, y: 2, z: 4, core: 2. Of those that a mesh axis runs over, the one named last changes fastest.
Arguments:
- qkv: bfloat16 [8192, 3, 2048], P('context', None, 'tensor'), may hold values from -6 to 6
- short_filter: float32 [7, 3, 2048], P(None, None, 'tensor'), may hold values from -2 to 2
- long_filter: float32 [128, 2048], P(None, 'tensor'), may hold values from -0.5 to 0.5
- out_weight: bfloat16 [2048, 2048], P('tensor'), may hold values from -0.125 to 0.125
- out_grad: bfloat16 [8192, 2048], P('context'), may hold values from -6 to 6
Outputs:
- output: bfloat16 [8192, 2048], P('context')
- qkv_grad: bfloat16 [8192, 3, 2048], P('context', None, 'tensor')
- long_grad: float32 [128, 2048], P(None, 'tensor')
- short_grad: float32 [7, 3, 2048], P(None, None, 'tensor')
- weight_grad: float32 [2048, 2048], P('context', 'tensor')
All inputs are finite; a program needn't handle non-finite values.
Results may differ from a plain program's by a relative error of at most 0.009.
Values may be sent and summed in bfloat16 or wider, within the bound.
A program may use at most 128 MiB of HBM per device.

v0:
```python
import jax
import jax.numpy as jnp
from jax import lax
from jax.sharding import PartitionSpec as P


def shifted(value, axis, steps):
    count = lax.axis_size(axis)
    leading, last = (max(0, -steps), min(count, count - steps))
    return lax.ppermute(value, axis, [(source, source + steps) for source in range(leading, last)])


def shortened(array):

    def short(part):
        return part.astype(jnp.bfloat16) if part.dtype == jnp.float32 else part

    return jax.tree.map(short, array)


def causal_conv(extended, lag_taps):
    kernel = lag_taps[::-1][:, None, :]
    result = lax.conv_general_dilated(
        extended[None],
        kernel,
        (1,),
        "VALID",
        dimension_numbers=("NWC", "WIO", "NWC"),
        feature_group_count=extended.shape[1],
        precision=lax.Precision.HIGHEST,
    )
    return result[0]


def reverse_conv(extended, lag_taps):
    kernel = lag_taps[:, None, :]
    result = lax.conv_general_dilated(
        extended[None],
        kernel,
        (1,),
        "VALID",
        dimension_numbers=("NWC", "WIO", "NWC"),
        feature_group_count=extended.shape[1],
        precision=lax.Precision.HIGHEST,
    )
    return result[0]


def lag_sums(extended, signal):
    result = lax.conv_general_dilated(
        extended[None],
        signal[:, None, :],
        (1,),
        "VALID",
        dimension_numbers=("NWC", "WIO", "NWC"),
        feature_group_count=extended.shape[1],
        precision=lax.Precision.HIGHEST,
    )
    return result[0][::-1]


def causal_half(extended, lag_taps):
    kernel = lag_taps[::-1][:, None, :]
    result = lax.conv_general_dilated(
        extended[None],
        kernel,
        (1,),
        "VALID",
        dimension_numbers=("NWC", "WIO", "NWC"),
        feature_group_count=extended.shape[1],
        preferred_element_type=jnp.float32,
    )
    return result[0]


def reverse_half(extended, lag_taps):
    kernel = lag_taps[:, None, :]
    result = lax.conv_general_dilated(
        extended[None],
        kernel,
        (1,),
        "VALID",
        dimension_numbers=("NWC", "WIO", "NWC"),
        feature_group_count=extended.shape[1],
        preferred_element_type=jnp.float32,
    )
    return result[0]


def lag_half(extended, signal):
    result = lax.conv_general_dilated(
        extended[None],
        signal[:, None, :],
        (1,),
        "VALID",
        dimension_numbers=("NWC", "WIO", "NWC"),
        feature_group_count=extended.shape[1],
        preferred_element_type=jnp.float32,
    )
    return result[0][::-1]


def shards(qkv, short_filter, long_filter, out_weight, out_grad):
    n_rows = qkv.shape[0]
    n_chans = qkv.shape[2]
    n_taps = long_filter.shape[0]
    n_short = short_filter.shape[0]
    width = 3 * n_chans
    short_taps = short_filter.reshape(n_short, width)
    long_taps = long_filter.astype(jnp.bfloat16)
    own_rows = qkv.astype(jnp.float32).reshape(n_rows, width)
    reach = n_taps + n_short - 2
    earlier = shifted(qkv[n_rows - reach :], "context", 1)
    widened = jnp.concatenate([earlier.astype(jnp.float32).reshape(reach, width), own_rows], axis=0)
    smoothed = causal_conv(widened, short_taps).reshape(n_rows + n_taps - 1, 3, n_chans)
    lagged = (smoothed[:, 1] * smoothed[:, 2]).astype(jnp.bfloat16)
    extended = widened[n_taps - 1 :]
    smoothed = smoothed[n_taps - 1 :]
    query_s = smoothed[:, 0]
    key_s = smoothed[:, 1]
    value_s = smoothed[:, 2]
    long_out = causal_half(lagged, long_taps)
    mixed = (query_s * long_out).astype(jnp.bfloat16)
    partial_value = jnp.dot(mixed, out_weight, preferred_element_type=jnp.float32)
    output = lax.psum(partial_value.astype(jnp.bfloat16), "tensor")
    mixed_grad = lax.dot_general(
        out_grad, out_weight, (((1,), (1,)), ((), ())), preferred_element_type=jnp.float32
    )
    weight_grad = lax.psum_scatter(
        lax.dot_general(
            out_grad, mixed, (((0,), (0,)), ((), ())), preferred_element_type=jnp.float32
        ),
        "context",
        scatter_dimension=0,
        tiled=True,
    )
    long_out_grad = (mixed_grad * query_s).astype(jnp.bfloat16)
    query_grad = mixed_grad * long_out
    later_grad = shifted(long_out_grad[: n_taps - 1], "context", -1)
    product_grad = reverse_half(jnp.concatenate([long_out_grad, later_grad], axis=0), long_taps)
    smoothed_grad = jnp.stack(
        [query_grad, product_grad * value_s, product_grad * key_s], axis=1
    ).reshape(n_rows, width)
    later_short = shifted(shortened(smoothed_grad[: n_short - 1]), "context", -1)
    qkv_grad = (
        reverse_conv(jnp.concatenate([smoothed_grad, later_short], axis=0), short_taps)
        .reshape(n_rows, 3, n_chans)
        .astype(jnp.bfloat16)
    )
    long_local = lag_half(lagged, long_out_grad)
    short_local = lag_sums(extended, smoothed_grad).reshape(n_short, 3, n_chans)
    long_grad, short_grad = lax.psum((long_local, short_local), "context")
    return (output, qkv_grad, long_grad, short_grad, weight_grad)


def solution(mesh):
    in_specs = (
        P("context", None, "tensor"),
        P(None, None, "tensor"),
        P(None, "tensor"),
        P("tensor", None),
        P("context", None),
    )
    out_specs = (
        P("context", None),
        P("context", None, "tensor"),
        P(None, "tensor"),
        P(None, None, "tensor"),
        P("context", "tensor"),
    )
    return jax.shard_map(shards, mesh=mesh, in_specs=in_specs, out_specs=out_specs, check_vma=False)
```

profile of v0, /device:TPU:0, one launch (start us, length us, event | category | flops | bytes accessed | tf_op | source)
XLA Modules:
  0.0 474.4 jit_solution(7967462110396242512)
XLA Ops:
  8.5 5.6 %collective-permute-start = (bf16[133,3,512]{2,0,1:T(8,128)(2,1)S(1)}, bf16[133,3,512]{2,0,1:T(8,128)(2,1)}, u32[]{:S(2)}, u32[]{:S(2)}) collective-permute-start(bf16[133,3,512]{2,0,1:T(8,128)(2,1)S(1)} %slice.35), channel_id=1, source_target_pairs={{0,4},{4,8},{8,12},{12,16},{16,20},{20,24},{24,28},{1,5},{5,9},{9,... | collective-permute-start | bytes 1225736 | tf_op jit(solution)/shard_map/ppermute | solution.py:10
  14.2 4.6 copy.21
  23.6 4.3 fusion.8
  30.1 12.5 %reshape.100 = bf16[1,8,145,1536]{2,1,3,0:T(8,128)(2,1)} reshape(bf16[1,1160,1536]{1,2,0:T(8,128)(2,1)} %pad) | data formatting | bytes 7127040 | tf_op jit(solution)/shard_map/conv_general_dilated | solution.py:23
  42.6 9.2 %copy.25 = bf16[1,8,145,1536]{3,1,2,0:T(8,128)(2,1)} copy(bf16[1,8,145,1536]{2,1,3,0:T(8,128)(2,1)} %reshape.100) | data formatting | bytes 7127040 | tf_op jit(solution)/shard_map/conv_general_dilated | solution.py:23
  52.8 8.2 %convolution_select_fusion = f32[8,145,1536]{2,0,1:T(8,128)S(1)} fusion(f32[7,1,1536]{2,1,0:T(1,128)S(1)} %broadcast_in_dim.27, bf16[1,7,6,1536]{3,1,2,0:T(8,128)(2,1)S(1)} %slice.55, bf16[1,8,145,1536]{3,1,2,0:T(8,128)(2,1)} %copy.25, pred[8,145]{0,1:T(8,128)(4,1)S(1)} %copy-done.17), kind=kOutput, calls=%fused_computation.16 | convolution fusion | flops 162582528 | bytes 10863752 | tf_op jit(solution)/shard_map/conv_general_dilated | solution.py:23
  61.0 7.1 %copy.26 = f32[8,145,1536]{2,1,0:T(8,128)} copy(f32[8,145,1536]{2,0,1:T(8,128)S(1)} %convolution_select_fusion) | data formatting | bytes 14254080 | tf_op jit(solution)/shard_map/conv_general_dilated | solution.py:23
  68.1 7.2 %reshape.66 = f32[1,1160,1536]{2,1,0:T(8,128)} reshape(f32[8,145,1536]{2,1,0:T(8,128)} %copy.26) | data formatting | bytes 14254080 | tf_op jit(solution)/shard_map/conv_general_dilated | solution.py:23
  75.4 6.6 %slice.58 = f32[1,1151,1536]{2,1,0:T(8,128)} slice(f32[1,1160,1536]{2,1,0:T(8,128)} %reshape.66), slice={[0:1], [0:1151], [0:1536]} | slice | bytes 14143488 | tf_op jit(solution)/shard_map/conv_general_dilated | solution.py:23
  85.3 8.1 %copy.28 = f32[1,1151,1536]{1,2,0:T(8,128)} copy(f32[1,1151,1536]{2,1,0:T(8,128)} %slice.58) | data formatting | bytes 14143488 | tf_op jit(solution)/shard_map/conv_general_dilated | solution.py:23
  100.2 60.3 %fusion.44 = f32[8,144,512]{2,0,1:T(8,128)S(1)} fusion(pred[8,144]{0,1:T(8,128)(4,1)S(1)} %copy-done.18, bf16[128,1,512]{2,0,1:T(8,128)(2,1)S(1)} %bitcast.109, bf16[8,271,512]{2,0,1:T(8,128)(2,1)S(1)} %fusion.80), kind=kOutput, calls=%fused_computation.56 | convolution fusion | flops 151584768 | bytes 4711552 | tf_op jit(solution)/shard_map/conv_general_dilated | solution.py:64
  166.3 6.7 %copy.27 = f32[1,1024,1536]{1,2,0:T(8,128)} copy(f32[1,1024,1536]{2,1,0:T(8,128)} %slice.56) | data formatting | bytes 12582912 | tf_op jit(solution)/shard_map/slice | solution.py:118
  173.0 7.4 %multiply_convert_fusion = (bf16[1024,512]{0,1:T(8,128)(2,1)S(1)}, bf16[1024,512]{0,1:T(8,128)(2,1)S(1)}, f32[1024,1,512]{0,2,1:T(8,128)}) fusion(f32[1024,3,512]{0,2,1:T(8,128)} %bitcast.94, f32[1,1024,512]{1,2,0:T(8,128)} %copy.64, bf16[1024,2048]{1,0:T(8,128)(2,1)} %param.9, bf16[512,2048]{1,0:T(8,128)(2,1)S(1)} %copy-done), kind=kOutput, calls=%fused_computation.53 | convolution fusion | flops 2150105088 | bytes 14680064 | tf_op jit(solution)/shard_map/dot_general | solution.py:126
  181.4 4.3 convolution_bitcast_fusion
  187.8 3.9 copy.49
  191.7 28.5 %fusion.22 = f32[1,128,512]{2,0,1:T(1,128)S(1)} fusion(bf16[1024,1,512]{2,1,0:T(2,128)(2,1)} %copy.49, bf16[1,1151,512]{2,1,0:T(8,128)(2,1)} %bitcast.103), kind=kOutput, calls=%fused_computation.32 | convolution fusion | flops 134217728 | bytes 2489344 | tf_op jit(solution)/shard_map/conv_general_dilated | solution.py:91
  221.5 4.4 fusion.18
  226.2 5.6 %convolution_convert_fusion = bf16[1024,2048]{1,0:T(8,128)(2,1)} fusion(bf16[1024,512]{0,1:T(8,128)(2,1)} %copy-done.21, bf16[512,2048]{1,0:T(8,128)(2,1)S(1)} %copy-done), kind=kOutput, calls=%fused_computation.19 | convolution fusion | flops 2149580800 | bytes 7340032 | tf_op jit(solution)/shard_map/dot_general | solution.py:124
  231.9 16.4 %copy.51 = bf16[1,1030,1536]{2,0,1:T(2,128)(2,1)} copy(bf16[1,1030,1536]{1,2,0:T(8,128)(2,1)} %fusion.18) | data formatting | bytes 6328320 | tf_op jit(solution)/shard_map/broadcast_in_dim | solution.py:51
  251.9 60.3 %fusion.41 = f32[8,144,512]{2,0,1:T(8,128)S(1)} fusion(pred[8,144]{0,1:T(8,128)(4,1)S(1)} %copy-done.19, bf16[128,1,512]{2,0,1:T(8,128)(2,1)S(1)} %copy-done.12, bf16[8,271,512]{2,0,1:T(8,128)(2,1)S(1)} %fusion.78), kind=kOutput, calls=%fused_computation.55 | convolution fusion | flops 151584768 | bytes 4711552 | tf_op jit(solution)/shard_map/conv_general_dilated | solution.py:78
  323.9 6.6 %copy.42 = f32[1024,1536]{1,0:T(8,128)} copy(f32[1024,1536]{0,1:T(8,128)} %bitcast.89) | data formatting | bytes 12582912 | tf_op jit(solution)/shard_map/reshape | solution.py:143
  332.0 16.0 %copy.52 = f32[1024,1,1536]{2,1,0:T(1,128)} copy(f32[1024,1,1536]{0,2,1:T(8,128)} %bitcast.90) | data formatting | bytes 12582912 | tf_op jit(solution)/shard_map/broadcast_in_dim;reshape | solution.py:52
  347.9 22.8 %fusion.64 = f32[1,7,1536]{2,0,1:T(1,128)S(1)} fusion(bf16[1,1030,1536]{2,0,1:T(2,128)(2,1)} %copy.51, f32[1024,1,1536]{2,1,0:T(1,128)} %copy.52), kind=kOutput, calls=%fused_computation.78 | convolution fusion | flops 132120576 | bytes 9498624 | tf_op jit(solution)/shard_map/conv_general_dilated | solution.py:50
  371.2 42.6 %psum.23 = f32[7,3,512]{2,1,0:T(4,128)S(1)} all-reduce(f32[7,3,512]{2,1,0:T(4,128)S(1)} %reshape.59), channel_id=1, replica_groups=mesh['context'=8,'tensor'=4] {'context'}, use_global_device_ids=true, to_apply=%region_2.0 | all-reduce | flops 10752 | bytes 86016 | tf_op jit(solution)/shard_map/psum | solution.py:152
  420.9 6.4 %reshape.83 = f32[1,8,129,1536]{3,2,1,0:T(8,128)} reshape(f32[1,1032,1536]{2,1,0:T(8,128)} %pad.6) | data formatting | bytes 12681216 | tf_op jit(solution)/shard_map/conv_general_dilated | solution.py:37
  427.3 6.6 %copy.44 = f32[1,8,129,1536]{3,1,2,0:T(8,128)S(1)} copy(f32[1,8,129,1536]{3,2,1,0:T(8,128)} %reshape.83) | data formatting | bytes 12681216 | tf_op jit(solution)/shard_map/conv_general_dilated | solution.py:37
  434.0 5.4 %select_convert_fusion = bf16[8,129,1536]{2,0,1:T(8,128)(2,1)S(1)} fusion(f32[1,7,6,1536]{3,1,2,0:T(8,128)S(1)} %slice.69, f32[1,8,129,1536]{3,1,2,0:T(8,128)S(1)} %copy.44, pred[8,129]{0,1:T(8,128)(4,1)S(1)} %copy-done.20, f32[7,1,1536]{2,0,1:T(8,128)S(1)} %bitcast.111), kind=kOutput, calls=%fused_computation.9 | convolution fusion | flops 141299712 | bytes 9813000 | tf_op jit(solution)/shard_map/conv_general_dilated | solution.py:37
  442.1 4.6 reshape.87
  446.7 3.8 slice.70
  450.4 4.7 copy.47
  455.1 4.6 copy.53
  461.9 4.8 %copy.82 = bf16[1024,2048]{1,0:T(8,128)(2,1)} copy(bf16[1024,2048]{1,0:T(8,128)(2,1)} %all-reduce.3.cloned.1.call-done) | data formatting | bytes 8388608
  (104 shorter events, 59.5 us)
Async XLA Ops:
  7.2 165.8 %copy-start = (bf16[512,2048]{1,0:T(8,128)(2,1)S(1)}, bf16[512,2048]{1,0:T(8,128)(2,1)}, u32[]{:S(2)}) copy-start(bf16[512,2048]{1,0:T(8,128)(2,1)} %param.8) | copy-start | bytes 6291460
  7.2 11.6 %copy-start.14 = (f32[7,3,512]{2,0,1:T(8,128)S(1)}, f32[7,3,512]{2,0,1:T(8,128)}, u32[]{:S(2)}) copy-start(f32[7,3,512]{2,0,1:T(8,128)} %param.6) | copy-start | bytes 129028
  7.2 11.9 %copy-start.10 = (f32[128,512]{1,0:T(8,128)S(1)}, f32[128,512]{1,0:T(8,128)}, u32[]{:S(2)}) copy-start(f32[128,512]{1,0:T(8,128)} %param.7) | copy-start | bytes 786436
  7.2 452.5 %reduce-scatter.2.cloned.1.call-start = ((), (), s32[]{:S(2)}) async-start(), calls=%async_computation.3 | async-start | bytes 4718592 | tf_op jit(solution)/shard_map/reduce_scatter | solution.py:129
  8.5 13.8 %collective-permute-start = (bf16[133,3,512]{2,0,1:T(8,128)(2,1)S(1)}, bf16[133,3,512]{2,0,1:T(8,128)(2,1)}, u32[]{:S(2)}, u32[]{:S(2)}) collective-permute-start(bf16[133,3,512]{2,0,1:T(8,128)(2,1)S(1)} %slice.35), channel_id=1, source_target_pairs={{0,4},{4,8},{8,12},{12,16},{16,20},{20,24},{24,28},{1,5},{5,9},{9,... | collective-permute-start | bytes 1225736 | tf_op jit(solution)/shard_map/ppermute | solution.py:10
  23.6 4.3 copy-start.4
  42.6 10.2 %copy-start.17 = (pred[8,145]{0,1:T(8,128)(4,1)S(1)}, pred[8,145]{0,1:T(8,128)(4,1)}, u32[]{:S(2)}) copy-start(pred[8,145]{0,1:T(8,128)(4,1)} %constant.28) | copy-start | bytes 3484
  75.4 6.6 %copy-start.3 = (f32[1,1160,1536]{2,1,0:T(8,128)S(1)}, f32[1,1160,1536]{2,1,0:T(8,128)}, u32[]{:S(2)}) copy-start(f32[1,1160,1536]{2,1,0:T(8,128)} %reshape.66) | copy-start | bytes 21381124
  98.5 1.3 copy-start.8
  99.3 0.9 copy-start.13
  99.3 0.9 copy-start.18
  173.0 8.4 %copy-start.16 = (bf16[1024,2048]{1,0:T(8,128)(2,1)S(1)}, bf16[1024,2048]{1,0:T(8,128)(2,1)}, u32[]{:S(2)}) copy-start(bf16[1024,2048]{1,0:T(8,128)(2,1)} %param.9) | copy-start | bytes 12582916
  180.4 1.0 copy-start.21
  180.4 7.4 %copy-start.6 = (bf16[1024,512]{0,1:T(8,128)(2,1)}, bf16[1024,512]{0,1:T(8,128)(2,1)S(1)}, u32[]{:S(2)}) copy-start(bf16[1024,512]{0,1:T(8,128)(2,1)S(1)} %get-tuple-element.17) | copy-start | bytes 3145732
  185.7 276.2 %all-reduce.5.cloned.1.call-start = ((), (), s32[]{:S(2)}) async-start(), calls=%async_computation.2 | async-start | bytes 524288 | tf_op jit(solution)/shard_map/psum | solution.py:152
  186.5 61.8 %collective-permute-start.1 = (bf16[127,512]{0,1:T(8,128)(2,1)S(1)}, bf16[127,512]{0,1:T(8,128)(2,1)S(1)}, u32[]{:S(2)}, u32[]{:S(2)}) collective-permute-start(bf16[127,512]{0,1:T(8,128)(2,1)S(1)} %slice.63), channel_id=1, source_target_pairs={{4,0},{8,4},{12,8},{16,12},{20,16},{24,20},{28,24},{5,1},{9,5},{13... | collective-permute-start | bytes 390152 | tf_op jit(solution)/shard_map/ppermute | solution.py:10
  191.7 29.8 %copy-start.5 = (bf16[133,3,512]{0,2,1:T(8,128)(2,1)S(1)}, bf16[133,3,512]{0,2,1:T(8,128)(2,1)}, u32[]{:S(2)}) copy-start(bf16[133,3,512]{0,2,1:T(8,128)(2,1)} %copy-done.4) | copy-start | bytes 1225732
  226.0 235.9 %all-reduce.3.cloned.1.call-start = ((), (), s32[]{:S(2)}) async-start(), calls=%async_computation.1 | async-start | bytes 8388608 | tf_op jit(solution)/shard_map/psum | solution.py:125
  248.3 1.2 copy-start.7
  251.0 0.9 copy-start.12
  251.0 0.9 copy-start.19
  317.0 3.1 copy-start.9
  321.2 2.6 copy-start.2
  330.7 83.8 %collective-permute-start.2 = (bf16[6,1536]{1,0:T(8,128)(2,1)S(1)}, bf16[6,1536]{1,0:T(8,128)(2,1)S(1)}, u32[]{:S(2)}, u32[]{:S(2)}) collective-permute-start(bf16[6,1536]{1,0:T(8,128)(2,1)S(1)} %copy.41), channel_id=1, source_target_pairs={{4,0},{8,4},{12,8},{16,12},{20,16},{24,20},{28,24},{5,1},{9,5},{13... | collective-permute-start | bytes 55304 | tf_op jit(solution)/shard_map/ppermute | solution.py:10
  427.3 6.7 %copy-start.15 = (f32[7,3,512]{2,0,1:T(8,128)S(1)}, f32[7,3,512]{2,0,1:T(8,128)}, u32[]{:S(2)}) copy-start(f32[7,3,512]{2,0,1:T(8,128)} %param.6) | copy-start | bytes 129028
  427.3 6.7 %copy-start.20 = (pred[8,129]{0,1:T(8,128)(4,1)S(1)}, pred[8,129]{0,1:T(8,128)(4,1)}, u32[]{:S(2)}) copy-start(pred[8,129]{0,1:T(8,128)(4,1)} %constant.30) | copy-start | bytes 3100
  459.7 7.7 %copy-start.1 = (bf16[512,2048]{1,0:T(8,128)(2,1)S(1)}, bf16[512,2048]{1,0:T(8,128)(2,1)}, u32[]{:S(2)}) copy-start(bf16[512,2048]{1,0:T(8,128)(2,1)} %param.8) | copy-start | bytes 6291460
  461.9 4.8 %copy-start.11 = (f32[128,512]{1,0:T(8,128)S(1)}, f32[128,512]{1,0:T(8,128)}, u32[]{:S(2)}) copy-start(f32[128,512]{1,0:T(8,128)} %all-reduce.5.cloned.1.call-done) | copy-start | bytes 786436
Sparse Core Ops, SparseCore 0:
  185.8 90.7 reduce-scatter.1
  281.0 70.2 all-reduce.4
  354.2 84.7 all-reduce.2
where the time goes:
time: 482 us; the launch traced here: 474 us
  matrix products  203 us (42%)
  local copies, waits for them, and re-layouts  183 us (38%)
  blocking collectives  42.6 us (9%)
  other arithmetic  21.1 us (4%)
  between operations  14.6 us (3%)
  starting transfers between devices  8.55 us (2%)
    conv_general_dilated x1, matrix products, reverse_half(): lax.conv_general_dilated(extended[None], kernel, (1,), 'VALID', dimension...  60.3 us
    conv_general_dilated x1, matrix products, causal_half(): lax.conv_general_dilated(extended[None], kernel, (1,), 'VALID', dimension...  60.3 us
    conv_general_dilated x7, local copies, waits for them, and re-layouts, causal_conv(): lax.conv_general_dilated(extended[None], kernel, (1,), 'VALID', dimension...  51.7 us
    psum x1, blocking collectives, shards(): long_grad, short_grad = lax.psum((long_local, short_local), 'context')  42.6 us
    unnamed x55, local copies, waits for them, and re-layouts  28.6 us
    conv_general_dilated x1, matrix products, lag_half(): lax.conv_general_dilated(extended[None], signal[:, None, :], (1,), 'VALID...  28.5 us
    conv_general_dilated x1, matrix products, lag_sums(): lax.conv_general_dilated(extended[None], signal[:, None, :], (1,), 'VALID...  22.8 us
    broadcast_in_dim x1, local copies, waits for them, and re-layouts, lag_sums(): extended[None]  16.4 us
  transfers between devices with their start and end apart: 6, of which 1 were waited for; matrix products, arithmetic and copies ran while one was open for 49% of the time, Pallas kernels for 0%

commit v1 on v0

v1 whole, which is shorter than its diff:
```python
import functools

import jax
import jax.numpy as jnp
import numpy as np
from jax import lax
from jax.experimental import pallas as pl
from jax.experimental.pallas import tpu as pltpu
from jax.sharding import PartitionSpec as P

BF = jnp.bfloat16
F32 = jnp.float32


def halves(array):
    high = np.asarray(array, np.float32).astype(jnp.bfloat16)
    low = (np.asarray(array, np.float32) - high.astype(np.float32)).astype(jnp.bfloat16)
    return high, low


def transforms(taps):
    n = 2 * taps
    angle = 2 * np.pi * np.outer(np.arange(taps) + 0.5, np.arange(n)) / n
    forward = np.concatenate([np.cos(angle), -np.sin(angle)], axis=0)
    inverse = np.concatenate([np.cos(angle), -np.sin(angle)], axis=0).T * (2.0 / n)
    return [jnp.asarray(part) for part in halves(forward) + halves(inverse)]


def mm(a, b):
    return jnp.dot(a, b, preferred_element_type=F32)


def split(value):
    high = value.astype(BF)
    return high, (value - high.astype(F32)).astype(BF)


def inverse_of(high_m, low_m, value):
    high, low = split(value)
    return mm(high_m, high) + (mm(high_m, low) + mm(low_m, high))


def times(a, b, n, conj):
    ar, ai, br, bi = a[:n], a[n:], b[:n], b[n:]
    if conj:
        return jnp.concatenate([ar * br + ai * bi, ai * br - ar * bi], axis=0)
    return jnp.concatenate([ar * br - ai * bi, ar * bi + ai * br], axis=0)


def first_kernel(n, pad, s, og, w, qkv, halo, short, longf, fh, fl, ih, il,
                 mixed, g_out, dq_out, ks_out, vs_out, lg, ext, prod, spec):
    rows = qkv.shape[1]
    top = n + pad
    for k in range(3):
        ext[k, 0:top, :] = halo[k].astype(F32)
        ext[k, top:, :] = qkv[k].astype(F32)
    h = longf[...].astype(BF)
    spec[...] = mm(fh[:, :n], h) + mm(fl[:, :n], h)
    lg[...] = jnp.zeros_like(lg)

    def smooth(k, e):
        window = ext[k, pl.ds(e, n + pad), :]
        total = short[k, 0:1, :] * window[pad:]
        for j in range(1, s):
            total = total + short[k, j:j + 1, :] * window[pad - j:pad - j + n]
        return total

    prod[0:n, :] = (smooth(1, 0) * smooth(2, 0)).astype(BF)

    def step(c, total):
        t = pl.multiple_of(c * n, n)
        e = pl.multiple_of(c * n + n, n)
        ks = smooth(1, e)
        vs = smooth(2, e)
        ks_out[pl.ds(t, n), :] = ks
        vs_out[pl.ds(t, n), :] = vs
        prod[pl.ds(e, n), :] = (ks * vs).astype(BF)
        qs = smooth(0, e)
        mg = lax.dot_general(og[pl.ds(t, n), :], w[...], (((1,), (1,)), ((), ())), preferred_element_type=F32)
        window = prod[pl.ds(t, 2 * n), :]
        x = mm(fh[...], window) + mm(fl[...], window)
        y = inverse_of(ih[n:, :], il[n:, :], times(x, spec[...], n, False))
        mixed[pl.ds(t, n), :] = (qs * y).astype(BF)
        g = (mg * qs).astype(BF)
        g_out[pl.ds(t, n), :] = g
        dq_out[pl.ds(t, n), :] = mg * y
        gs = mm(fh[:, n:], g) + mm(fl[:, n:], g)
        return total + times(gs, x, n, True)

    total = lax.fori_loop(0, rows // n, step, jnp.zeros((2 * n, w.shape[0]), F32))
    lg[...] = inverse_of(ih[:n, :], il[:n, :], total)


def second_kernel(n, pad, s, g, tail, dq, ks, vs, qkv, halo, short, longf, fh, fl, ih, il,
                  grad, sg, ext, gext, spec, sums):
    rows = qkv.shape[1]
    for k in range(3):
        ext[k, 0:pad, :] = halo[k, n:n + pad, :].astype(F32)
        ext[k, pad:, :] = qkv[k].astype(F32)
    gext[0:rows, :] = g[...]
    gext[rows:rows + n + 16, :] = tail[0:n + 16, :]
    gext[rows + n + 16:, :] = jnp.zeros((n - 16, g.shape[1]), BF)
    h = longf[...].astype(BF)
    spec[...] = mm(fh[:, :n], h) + mm(fl[:, :n], h)
    sums[...] = jnp.zeros_like(sums)

    def long_back(t):
        window = gext[pl.ds(t, 2 * n), :]
        x = mm(fh[...], window) + mm(fl[...], window)
        return inverse_of(ih[:n, :], il[:n, :], times(x, spec[...], n, True))

    pg = long_back(rows)[:pad]
    heads = (
        tail[n + 16:n + 16 + pad, :].astype(F32),
        pg * tail[n + 48:n + 48 + pad, :].astype(F32),
        pg * tail[n + 32:n + 32 + pad, :].astype(F32),
    )

    def step(i, heads):
        t = pl.multiple_of(rows - n - i * n, n)
        pg = long_back(t)
        owns = (dq[pl.ds(t, n), :], pg * vs[pl.ds(t, n), :], pg * ks[pl.ds(t, n), :])
        for k in range(3):
            own = owns[k]
            window = jnp.concatenate([own, heads[k]], axis=0)
            raw = ext[k, pl.ds(t, n + pad), :]
            total = short[k, 0:1, :] * own
            for j in range(s):
                if j:
                    total = total + short[k, j:j + 1, :] * window[j:j + n]
                term = own * raw[pad - j:pad - j + n]
                sums[k, j] += jnp.sum(term.reshape(n // 8, 8, term.shape[1]), axis=0)
            grad[k, pl.ds(t, n), :] = total.astype(BF)
        return tuple(own[:pad] for own in owns)

    lax.fori_loop(0, rows // n, step, heads)
    sg[...] = jnp.sum(sums[...], axis=2)


def shifted(value, axis, steps):
    count = lax.axis_size(axis)
    leading, last = (max(0, -steps), min(count, count - steps))
    return lax.ppermute(value, axis, [(source, source + steps) for source in range(leading, last)])


def shards(qkv, short_filter, long_filter, out_weight, out_grad):
    rows, _, chans = qkv.shape
    n, s, pad = long_filter.shape[0], short_filter.shape[0], 8
    feats = out_weight.shape[1]
    cb = 256
    streams = jnp.transpose(qkv, (1, 0, 2))
    short = jnp.transpose(short_filter, (1, 0, 2))
    halo = shifted(streams[:, rows - n - pad:], "context", 1)
    matrices = transforms(n)

    def by_chan(*lead):
        zeros = (0,) * len(lead)
        return pl.BlockSpec(lead + (cb,), lambda i: zeros + (i,))

    def whole(shape):
        zeros = (0,) * len(shape)
        return pl.BlockSpec(shape, lambda i: zeros)

    mats = [whole((2 * n, 2 * n))] * 4
    top = n + pad
    conv_flops = 40 * rows * n * chans
    params = pltpu.CompilerParams(vmem_limit_bytes=56 * 2**20)
    mixed, g, dq, ks, vs, long_local = pl.pallas_call(
        functools.partial(first_kernel, n, pad, s),
        grid=(chans // cb,),
        out_shape=[
            jax.ShapeDtypeStruct((rows, chans), BF),
            jax.ShapeDtypeStruct((rows, chans), BF),
            jax.ShapeDtypeStruct((rows, chans), F32),
            jax.ShapeDtypeStruct((rows, chans), F32),
            jax.ShapeDtypeStruct((rows, chans), F32),
            jax.ShapeDtypeStruct((n, chans), F32),
        ],
        in_specs=[
            whole((rows, feats)),
            pl.BlockSpec((cb, feats), lambda i: (i, 0)),
            by_chan(3, rows),
            by_chan(3, top),
            by_chan(3, s),
            by_chan(n),
        ] + mats,
        out_specs=[by_chan(rows)] * 5 + [by_chan(n)],
        scratch_shapes=[
            pltpu.VMEM((3, rows + top, cb), F32),
            pltpu.VMEM((rows + n, cb), BF),
            pltpu.VMEM((2 * n, cb), F32),
        ],
        compiler_params=params,
        cost_estimate=pl.CostEstimate(flops=2 * rows * chans * feats + conv_flops, bytes_accessed=20 * 2**20, transcendentals=0),
        name="forward",
    )(out_grad, out_weight, streams, halo, short, long_filter, *matrices)
    head = jnp.concatenate([g[:n + 16]] + [part[:16].astype(BF) for part in (dq, ks, vs)], axis=0)
    tail = shifted(head, "context", -1)
    partial_value = jnp.dot(mixed, out_weight, preferred_element_type=F32).astype(BF)
    output = lax.psum(partial_value, "tensor")
    weight_local = lax.dot_general(
        out_grad, mixed, (((0,), (0,)), ((), ())), preferred_element_type=F32
    ).astype(BF)
    weight_grad = lax.psum_scatter(weight_local, "context", scatter_dimension=0, tiled=True).astype(F32)
    g, tail, _ = lax.optimization_barrier((g, tail, weight_local))
    grad, short_local = pl.pallas_call(
        functools.partial(second_kernel, n, pad, s),
        grid=(chans // cb,),
        out_shape=[
            jax.ShapeDtypeStruct((3, rows, chans), BF),
            jax.ShapeDtypeStruct((3, s, chans), F32),
        ],
        in_specs=[by_chan(rows), by_chan(n + 64)] + [by_chan(rows)] * 3 + [
            by_chan(3, rows),
            by_chan(3, top),
            by_chan(3, s),
            by_chan(n),
        ] + mats,
        out_specs=[by_chan(3, rows), by_chan(3, s)],
        scratch_shapes=[
            pltpu.VMEM((3, rows + pad, cb), F32),
            pltpu.VMEM((rows + 2 * n, cb), BF),
            pltpu.VMEM((2 * n, cb), F32),
            pltpu.VMEM((3, s, 8, cb), F32),
        ],
        compiler_params=params,
        cost_estimate=pl.CostEstimate(flops=conv_flops * 4, bytes_accessed=20 * 2**20, transcendentals=0),
        name="backward",
    )(g, tail, dq, ks, vs, streams, halo, short, long_filter, *matrices)
    filters = jnp.concatenate([long_local, short_local.reshape(3 * s, chans)], axis=0)
    filters = lax.psum(filters, "context")
    long_grad = filters[:n]
    short_grad = jnp.transpose(filters[n:].reshape(3, s, chans), (1, 0, 2))
    return output, jnp.transpose(grad, (1, 0, 2)), long_grad, short_grad, weight_grad


def solution(mesh):
    in_specs = (
        P("context", None, "tensor"),
        P(None, None, "tensor"),
        P(None, "tensor"),
        P("tensor", None),
        P("context", None),
    )
    out_specs = (
        P("context", None),
        P("context", None, "tensor"),
        P(None, "tensor"),
        P(None, None, "tensor"),
        P("context", "tensor"),
    )
    return jax.shard_map(shards, mesh=mesh, in_specs=in_specs, out_specs=out_specs, check_vma=False)
```

time: 482 us -> 335 us (0.70); the launches traced: 474 us -> 335 us
  waiting for transfers between devices: 1.86 us -> 233 us
  matrix products: 203 us -> 10.5 us
  local copies, waits for them, and re-layouts: 183 us -> 16.3 us
  Pallas kernels: 0 us -> 54.1 us
  blocking collectives: 42.6 us -> 0 us
  other arithmetic: 21.1 us -> 0.76 us
    conv_general_dilated x6 -> x0, matrix products: 186 us -> none  [the longest x1 60.3 us: reverse_half(): lax.conv_general_dilated(extended[None], kernel, (1,), 'VALID', dimension...]
    psum x2, waiting for transfers between devices: 0.01 us -> 152 us  [the longest x1 85.7 us: shards(): output = lax.psum(partial_value, 'tensor')]
    conv_general_dilated x18 -> x0, local copies, waits for them, and re-layouts: 72.3 us -> none  [the longest x7 51.7 us: causal_conv(): lax.conv_general_dilated(extended[None], kernel, (1,), 'VALID', dimension...]
    reduce_scatter x1, waiting for transfers between devices: 0.01 us -> 68.6 us  [shards(): lax.psum_scatter(weight_local, 'context', scatter_dimension=0, tiled=True)]
    pallas_call x0 -> x2, Pallas kernels: none -> 54.1 us  [the longest x1 27.2 us: shards(): pl.pallas_call(functools.partial(first_kernel, n, pad, s), grid=(chans //...]
    psum x1 -> x0, blocking collectives: 42.6 us -> none  [shards(): long_grad, short_grad = lax.psum((long_local, short_local), 'context')]
    broadcast_in_dim x6 -> x0, local copies, waits for them, and re-layouts: 25.8 us -> none  [the longest x1 16.4 us: lag_sums(): extended[None]]
    unnamed x55 -> x12, local copies, waits for them, and re-layouts: 28.6 us -> 8.13 us
  transfers between devices with their start and end apart: 6 -> 5, of which waited for: 1 -> 5; matrix products, arithmetic and copies ran while one was open for 49% -> 5% of each run, Pallas kernels for 0% -> 0%
where the time goes in v1:
time: 335 us
  waiting for transfers between devices  233 us (70%)
  Pallas kernels  54.1 us (16%)
  local copies, waits for them, and re-layouts  16.3 us (5%)
  between operations  13.8 us (4%)
  matrix products  10.5 us (3%)
  starting transfers between devices  6.31 us (2%)
    psum x1, waiting for transfers between devices, shards(): output = lax.psum(partial_value, 'tensor')  85.7 us
    reduce_scatter x1, waiting for transfers between devices, shards(): lax.psum_scatter(weight_local, 'context', scatter_dimension=0, tiled=True)  68.6 us
    psum x1, waiting for transfers between devices, shards(): filters = lax.psum(filters, 'context')  66.7 us
    pallas_call x1, Pallas kernels, shards(): pl.pallas_call(functools.partial(first_kernel, n, pad, s), grid=(chans //...  27.2 us
    pallas_call x1, Pallas kernels, shards(): pl.pallas_call(functools.partial(second_kernel, n, pad, s), grid=(chans /...  26.9 us
    ppermute x2, waiting for transfers between devices, shifted(): lax.ppermute(value, axis, [(source, source + steps) for source in range(l...  11 us
    unnamed x12, local copies, waits for them, and re-layouts  8.13 us
  transfers between devices with their start and end apart: 5, of which 5 were waited for; matrix products, arithmetic and copies ran while one was open for 5% of the time, Pallas kernels for 0%

profile of v1, /device:TPU:0, one launch (start us, length us, event | category | flops | bytes accessed | tf_op | source)
XLA Modules:
  0.0 334.5 jit_solution(4466866787673402228)
XLA Ops:
  7.2 0.0 all-reduce.5.cloned.1.call-start
  7.2 1.0 slice.31
  8.3 4.9 %collective-permute-start = (bf16[3,136,512]{2,1,0:T(8,128)(2,1)S(1)}, bf16[3,136,512]{2,1,0:T(8,128)(2,1)S(1)}, u32[]{:S(2)}, u32[]{:S(2)}) collective-permute-start(bf16[3,136,512]{2,1,0:T(8,128)(2,1)S(1)} %slice.31), channel_id=1, source_target_pairs={{0,4},{4,8},{8,12},{12,16},{16,20},{20,24},{24,28},{1,5},{5,9},{9,... | collective-permute-start | bytes 1253384 | tf_op jit(solution)/shard_map/ppermute | solution.py:143
  13.2 8.9 %collective-permute-done.halo = bf16[3,136,512]{2,1,0:T(8,128)(2,1)S(1)} collective-permute-done((bf16[3,136,512]{2,1,0:T(8,128)(2,1)S(1)}, bf16[3,136,512]{2,1,0:T(8,128)(2,1)S(1)}, u32[]{:S(2)}, u32[]{:S(2)}) %collective-permute-start) | collective-permute-done | bytes 417824 | tf_op jit(solution)/shard_map/ppermute | solution.py:143
  22.0 0.8 copy-done.3
  22.8 27.2 %forward.1 = (bf16[1024,512]{1,0:T(8,128)(2,1)}, bf16[1024,512]{1,0:T(8,128)(2,1)}, f32[1024,512]{1,0:T(8,128)}, f32[1024,512]{1,0:T(8,128)}, f32[1024,512]{1,0:T(8,128)}, /*index=5*/f32[128,512]{1,0:T(8,128)}) custom-call(bf16[1024,2048]{1,0:T(8,128)(2,1)} %og.1, bf16[512,2048]{1,0:T(8,128)(2,1)} %w.1, bf16[3,1024,512]{2,1,0:T(8,128)(2,1)} %bitcast.11, ...), custom_call_target="tpu_custom_call" | custom-call | flops 4831838208 | bytes 20971520 | tf_op jit(solution)/shard_map/forward/pallas_call | solution.py:168
  50.0 0.8 slice.42
  50.8 0.8 slice.41
  51.5 0.8 slice.40
  52.3 0.9 slice.25
  53.2 1.3 collective-permute-start.1
  54.5 0.0 copy-done.1
  54.5 4.9 %fusion = bf16[2048,512]{0,1:T(8,128)(2,1)} fusion(bf16[1024,512]{1,0:T(8,128)(2,1)} %get-tuple-element.15, bf16[1024,2048]{1,0:T(8,128)(2,1)S(1)} %copy-done.1), kind=kOutput, calls=%fused_computation.2 | convolution fusion | flops 2148532224 | bytes 7340032 | tf_op jit(solution)/shard_map/dot_general | solution.py:201
  59.5 2.2 collective-permute-done.1.tail
  61.6 0.7 copy-done.4
  62.3 26.9 %backward.1 = (bf16[3,1024,512]{2,1,0:T(8,128)(2,1)}, f32[3,7,512]{2,1,0:T(8,128)}) custom-call(bf16[1024,512]{1,0:T(8,128)(2,1)} %get-tuple-element.20.g, bf16[192,512]{1,0:T(8,128)(2,1)} %copy-done.4, f32[1024,512]{1,0:T(8,128)} %get-tuple-element.17.dq, f32[1024,512]{1,0:T(8,128)} %get-tuple-element.18.ks, f32[1024,512]{1,0:T(8,128)} %get-tuple-element.19.vs, ...), custom_call_target="tpu_custom_call" | custom-call | flops 10737418240 | bytes 20971520 | tf_op jit(solution)/shard_map/backward/pallas_call | solution.py:206
  89.3 0.8 reshape.16
  90.1 0.7 pad_maximum_fusion
  90.8 0.0 all-reduce.5.cloned.1.call-update
  90.8 0.0 reduce-scatter.2.cloned.1.call-start
  90.9 0.7 reduce-scatter.2.cloned.1.call-update
  91.6 0.0 all-reduce.3.cloned.1.call-start
  91.6 5.6 %convolution_convert_fusion = bf16[1024,2048]{1,0:T(8,128)(2,1)} fusion(bf16[1024,512]{1,0:T(8,128)(2,1)} %get-tuple-element.15, bf16[512,2048]{1,0:T(8,128)(2,1)S(1)} %copy-done.2), kind=kOutput, calls=%fused_computation | convolution fusion | flops 2149580800 | bytes 7340032 | tf_op jit(solution)/shard_map/dot_general | solution.py:199
  97.2 0.0 all-reduce.3.cloned.1.call-update
  97.2 66.7 %all-reduce.5.cloned.1.call-done = f32[149,512]{1,0:T(8,128)} async-done(((f32[149,512]{1,0:T(8,128)}), f32[149,512]{1,0:T(8,128)}) %all-reduce.5.cloned.1.call-update) | async-done | bytes 305168 | tf_op jit(solution)/shard_map/psum | solution.py:231
  163.9 0.8 slice.36
  164.7 0.6 reshape.17
  165.3 1.7 slice.35
  167.0 68.6 %reduce-scatter.2.cloned.1.call-done = bf16[256,512]{0,1:T(8,128)(2,1)} async-done(((bf16[2048,512]{0,1:T(8,128)(2,1)}), bf16[256,512]{0,1:T(8,128)(2,1)}) %reduce-scatter.2.cloned.1.call-update) | async-done | bytes 262160 | tf_op jit(solution)/shard_map/reduce_scatter | solution.py:204
  235.6 1.9 copy.14
  237.5 85.7 %all-reduce.3.cloned.1.call-done = bf16[1024,2048]{1,0:T(8,128)(2,1)} async-done(((bf16[1024,2048]{1,0:T(8,128)(2,1)}), bf16[1024,2048]{1,0:T(8,128)(2,1)}) %all-reduce.3.cloned.1.call-update) | async-done | bytes 4194320 | tf_op jit(solution)/shard_map/psum | solution.py:200
  323.2 4.8 %copy.17 = bf16[1024,2048]{1,0:T(8,128)(2,1)} copy(bf16[1024,2048]{1,0:T(8,128)(2,1)} %all-reduce.3.cloned.1.call-done) | data formatting | bytes 8388608
  (8 shorter events, 0.0 us)
Async XLA Ops:
  7.2 156.8 %all-reduce.5.cloned.1.call-start = ((), (), s32[]{:S(2)}) async-start(), calls=%async_computation.2 | async-start | bytes 622592 | tf_op jit(solution)/shard_map/psum | solution.py:231
  8.3 13.8 %collective-permute-start = (bf16[3,136,512]{2,1,0:T(8,128)(2,1)S(1)}, bf16[3,136,512]{2,1,0:T(8,128)(2,1)S(1)}, u32[]{:S(2)}, u32[]{:S(2)}) collective-permute-start(bf16[3,136,512]{2,1,0:T(8,128)(2,1)S(1)} %slice.31), channel_id=1, source_target_pairs={{0,4},{4,8},{8,12},{12,16},{16,20},{20,24},{24,28},{1,5},{5,9},{9,... | collective-permute-start | bytes 1253384 | tf_op jit(solution)/shard_map/ppermute | solution.py:143
  22.0 0.8 copy-start.3
  22.8 31.8 %copy-start.1 = (bf16[1024,2048]{1,0:T(8,128)(2,1)S(1)}, bf16[1024,2048]{1,0:T(8,128)(2,1)}, u32[]{:S(2)}) copy-start(bf16[1024,2048]{1,0:T(8,128)(2,1)} %og.1) | copy-start | bytes 12582916
  53.2 8.4 %collective-permute-start.1 = (bf16[192,512]{1,0:T(8,128)(2,1)S(1)}, bf16[192,512]{1,0:T(8,128)(2,1)S(1)}, u32[]{:S(2)}, u32[]{:S(2)}) collective-permute-start(bf16[192,512]{1,0:T(8,128)(2,1)S(1)} %pad_maximum_fusion.1), channel_id=1, source_target_pairs={{4,0},{8,4},{12,8},{16,12},{20,16},{24,20},{28,24},{5,1},{9,5},{13... | collective-permute-start | bytes 589832 | tf_op jit(solution)/shard_map/ppermute | solution.py:143
  59.5 30.6 %copy-start = (f32[128,512]{1,0:T(8,128)S(1)}, f32[128,512]{1,0:T(8,128)}, u32[]{:S(2)}) copy-start(f32[128,512]{1,0:T(8,128)} %get-tuple-element.23) | copy-start | bytes 786436
  59.5 32.2 %copy-start.2 = (bf16[512,2048]{1,0:T(8,128)(2,1)S(1)}, bf16[512,2048]{1,0:T(8,128)(2,1)}, u32[]{:S(2)}) copy-start(bf16[512,2048]{1,0:T(8,128)(2,1)} %w.1) | copy-start | bytes 6291460
  61.6 0.7 copy-start.4
  90.8 144.8 %reduce-scatter.2.cloned.1.call-start = ((), (), s32[]{:S(2)}) async-start(), calls=%async_computation.3 | async-start | bytes 2359296 | tf_op jit(solution)/shard_map/reduce_scatter | solution.py:204
  91.6 231.6 %all-reduce.3.cloned.1.call-start = ((), (), s32[]{:S(2)}) async-start(), calls=%async_computation.1 | async-start | bytes 8388608 | tf_op jit(solution)/shard_map/psum | solution.py:200
Sparse Core Ops, SparseCore 0:
  91.0 72.9 all-reduce.4
  167.9 67.7 reduce-scatter.1
  238.7 84.4 all-reduce.2

commit v2 on v1

--- a/solution.py
+++ b/solution.py
@@ -143,6 +143,99 @@
     return lax.ppermute(value, axis, [(source, source + steps) for source in range(leading, last)])
 
 
+def sum_kernel(count, chunks, part, filt, out, total, near, mine, far, slots, sems, fsems):
+    mesh_id = pl.DeviceIdType.MESH
+    place = lax.axis_index("context")
+    member = lax.axis_index("tensor")
+    core = lax.rem(member, 2)
+    sibling = (place, member + 1 - 2 * core)
+    peer = (place, lax.rem(member + 2, 4))
+    others = [lax.rem(place + d, count) for d in range(1, count)]
+    half = part.shape[0] // 2
+    size = half // chunks
+    piece = filt.shape[0] // count
+
+    barrier = pltpu.get_barrier_semaphore()
+    for device in [sibling, peer] + [(other, member) for other in others]:
+        pl.semaphore_signal(barrier, inc=1, device_id=device, device_id_type=mesh_id)
+    pl.semaphore_wait(barrier, count + 1)
+
+    def send(source, target, pair, index, device):
+        copy = pltpu.make_async_remote_copy(
+            src_ref=source, dst_ref=target, send_sem=pair.at[0, index], recv_sem=pair.at[1, index],
+            device_id=device, device_id_type=mesh_id,
+        )
+        copy.start()
+        return copy
+
+    def own_rows(side, c):
+        return pl.ds(pl.multiple_of(side * half + c * size, size), size)
+
+    def rows_of(index):
+        return pl.ds(pl.multiple_of(index * piece, piece), piece)
+
+    first = [
+        send(part.at[own_rows(1 - core, c)], near.at[c], sems, c, sibling) for c in range(chunks)
+    ]
+    gather = [
+        send(filt.at[rows_of(other)], slots.at[d], fsems, d, (other, member)) for d, other in enumerate(others)
+    ]
+    second = []
+    for c in range(chunks):
+        first[c].wait_recv()
+        mine[c] = (part[own_rows(core, c), :].astype(F32) + near[c].astype(F32)).astype(BF)
+        second.append(send(mine.at[c], far.at[c], sems, chunks + c, peer))
+    for copy in gather:
+        copy.wait_recv()
+    value = filt[rows_of(place), :]
+    for d in range(count - 1):
+        value = value + slots[d]
+    total[rows_of(place), :] = value
+    spread = [
+        send(total.at[rows_of(place)], total.at[rows_of(place)], fsems, count - 1 + d, (other, member))
+        for d, other in enumerate(others)
+    ]
+    third = []
+    for c in range(chunks):
+        second[c].wait_recv()
+        out[own_rows(core, c), :] = (mine[c].astype(F32) + far[c].astype(F32)).astype(BF)
+        third.append(send(out.at[own_rows(core, c)], out.at[own_rows(core, c)], sems, 2 * chunks + c, sibling))
+    for copy in spread + third:
+        copy.wait_recv()
+    for copy in first + gather + second + spread + third:
+        copy.wait_send()
+
+
+def summed(partial_value, filters):
+    rows, feats = partial_value.shape
+    count = lax.axis_size("context")
+    length, chans = filters.shape
+    piece = -(-length // (8 * count)) * 8
+    filters = jnp.concatenate([filters, jnp.zeros((piece * count - length, chans), F32)], axis=0)
+    chunks = 4
+    size = rows // 2 // chunks
+    vmem = pl.BlockSpec(memory_space=pltpu.VMEM)
+    return pl.pallas_call(
+        functools.partial(sum_kernel, count, chunks),
+        out_shape=[
+            jax.ShapeDtypeStruct((rows, feats), BF),
+            jax.ShapeDtypeStruct((piece * count, chans), F32),
+        ],
+        in_specs=[vmem, vmem],
+        out_specs=[vmem, vmem],
+        scratch_shapes=[pltpu.VMEM((chunks, size, feats), BF)] * 3 + [
+            pltpu.VMEM((count - 1, piece, chans), F32),
+            pltpu.SemaphoreType.DMA((2, 3 * chunks)),
+            pltpu.SemaphoreType.DMA((2, 2 * (count - 1))),
+        ],
+        compiler_params=pltpu.CompilerParams(
+            collective_id=0, has_side_effects=True, vmem_limit_bytes=40 * 2**20
+        ),
+        cost_estimate=pl.CostEstimate(flops=6 * rows * feats, bytes_accessed=100 * 2**20, transcendentals=0),
+        name="sums",
+    )(partial_value, filters)
+
+
 def shards(qkv, short_filter, long_filter, out_weight, out_grad):
     rows, _, chans = qkv.shape
     n, s, pad = long_filter.shape[0], short_filter.shape[0], 8
@@ -197,7 +290,6 @@
     head = jnp.concatenate([g[:n + 16]] + [part[:16].astype(BF) for part in (dq, ks, vs)], axis=0)
     tail = shifted(head, "context", -1)
     partial_value = jnp.dot(mixed, out_weight, preferred_element_type=F32).astype(BF)
-    output = lax.psum(partial_value, "tensor")
     weight_local = lax.dot_general(
         out_grad, mixed, (((0,), (0,)), ((), ())), preferred_element_type=F32
     ).astype(BF)
@@ -228,9 +320,9 @@
         name="backward",
     )(g, tail, dq, ks, vs, streams, halo, short, long_filter, *matrices)
     filters = jnp.concatenate([long_local, short_local.reshape(3 * s, chans)], axis=0)
-    filters = lax.psum(filters, "context")
+    output, filters = summed(partial_value, filters)
     long_grad = filters[:n]
-    short_grad = jnp.transpose(filters[n:].reshape(3, s, chans), (1, 0, 2))
+    short_grad = jnp.transpose(filters[n:n + 3 * s].reshape(3, s, chans), (1, 0, 2))
     return output, jnp.transpose(grad, (1, 0, 2)), long_grad, short_grad, weight_grad
 
 

time: 335 us -> 173 us (0.52)
  waiting for transfers between devices: 233 us -> 11.7 us
  Pallas kernels: 54.1 us -> 112 us
    psum x2 -> x0, waiting for transfers between devices: 152 us -> none  [the longest x1 85.7 us: shards(): output = lax.psum(partial_value, 'tensor')]
    reduce_scatter x1, waiting for transfers between devices: 68.6 us -> 0.01 us  [shards(): lax.psum_scatter(weight_local, 'context', scatter_dimension=0, tiled=True)]
    pallas_call x0 -> x1, Pallas kernels: none -> 57.5 us  [summed(): pl.pallas_call(functools.partial(sum_kernel, count, chunks), out_shape=[j...]
    unnamed x12 -> x18, local copies, waits for them, and re-layouts: 8.13 us -> 12.3 us
  transfers between devices with their start and end apart: 5 -> 3, of which waited for: 5 -> 2; matrix products, arithmetic and copies ran while one was open for 5% -> 6% of each run, Pallas kernels for 0% -> 49%
where the time goes in v2:
time: 173 us; the launch traced here: 172 us
  Pallas kernels  112 us (65%)
  local copies, waits for them, and re-layouts  18.8 us (11%)
  between operations  14.2 us (8%)
  waiting for transfers between devices  11.7 us (7%)
  matrix products  9.55 us (6%)
  starting transfers between devices  6.23 us (4%)
    pallas_call x1, Pallas kernels, summed(): pl.pallas_call(functools.partial(sum_kernel, count, chunks), out_shape=[j...  57.5 us
    pallas_call x1, Pallas kernels, shards(): pl.pallas_call(functools.partial(first_kernel, n, pad, s), grid=(chans //...  27.2 us
    pallas_call x1, Pallas kernels, shards(): pl.pallas_call(functools.partial(second_kernel, n, pad, s), grid=(chans /...  26.9 us
    unnamed x18, local copies, waits for them, and re-layouts  12.3 us
    ppermute x2, waiting for transfers between devices, shifted(): lax.ppermute(value, axis, [(source, source + steps) for source in range(l...  11.7 us
    ppermute x2, starting transfers between devices, shifted(): lax.ppermute(value, axis, [(source, source + steps) for source in range(l...  6.19 us
    dot_general x1, matrix products, shards(): lax.dot_general(out_grad, mixed, (((0,), (0,)), ((), ())), preferred_elem...  5.15 us
    dot_general x1, matrix products, shards(): jnp.dot(mixed, out_weight, preferred_element_type=F32).astype(BF)  4.39 us
  transfers between devices with their start and end apart: 3, of which 2 were waited for; matrix products, arithmetic and copies ran while one was open for 6% of the time, Pallas kernels for 49%

profile of v2, /device:TPU:0, one launch (start us, length us, event | category | flops | bytes accessed | tf_op | source)
XLA Modules:
  0.0 172.2 jit_solution(15085781102768063308)
XLA Ops:
  7.2 0.0 reduce-scatter.2.cloned.1.call-start
  7.2 1.0 slice.31
  8.3 4.9 %collective-permute-start = (bf16[3,136,512]{2,1,0:T(8,128)(2,1)S(1)}, bf16[3,136,512]{2,1,0:T(8,128)(2,1)S(1)}, u32[]{:S(2)}, u32[]{:S(2)}) collective-permute-start(bf16[3,136,512]{2,1,0:T(8,128)(2,1)S(1)} %slice.31), channel_id=1, source_target_pairs={{0,4},{4,8},{8,12},{12,16},{16,20},{20,24},{24,28},{1,5},{5,9},{9,... | collective-permute-start | bytes 1253384 | tf_op jit(solution)/shard_map/ppermute | solution.py:143
  13.2 8.9 %collective-permute-done.halo = bf16[3,136,512]{2,1,0:T(8,128)(2,1)S(1)} collective-permute-done((bf16[3,136,512]{2,1,0:T(8,128)(2,1)S(1)}, bf16[3,136,512]{2,1,0:T(8,128)(2,1)S(1)}, u32[]{:S(2)}, u32[]{:S(2)}) %collective-permute-start) | collective-permute-done | bytes 417824 | tf_op jit(solution)/shard_map/ppermute | solution.py:143
  22.0 0.8 copy-done.5
  22.8 27.2 %forward.1 = (bf16[1024,512]{1,0:T(8,128)(2,1)}, bf16[1024,512]{1,0:T(8,128)(2,1)}, f32[1024,512]{1,0:T(8,128)}, f32[1024,512]{1,0:T(8,128)}, f32[1024,512]{1,0:T(8,128)}, /*index=5*/f32[128,512]{1,0:T(8,128)}) custom-call(bf16[1024,2048]{1,0:T(8,128)(2,1)} %og.1, bf16[512,2048]{1,0:T(8,128)(2,1)} %w.1, bf16[3,1024,512]{2,1,0:T(8,128)(2,1)} %bitcast.11, ...), custom_call_target="tpu_custom_call" | custom-call | flops 4831838208 | bytes 20971520 | tf_op jit(solution)/shard_map/forward/pallas_call | solution.py:261
  50.0 0.0 copy-done.3
  50.0 0.0 copy-start.4
  50.0 0.0 copy-start.7
  50.0 5.2 %fusion = bf16[2048,512]{0,1:T(8,128)(2,1)} fusion(bf16[1024,512]{1,0:T(8,128)(2,1)} %get-tuple-element.17, bf16[1024,2048]{1,0:T(8,128)(2,1)S(1)} %copy-done.3), kind=kOutput, calls=%fused_computation.2 | convolution fusion | flops 2148532224 | bytes 7340032 | tf_op jit(solution)/shard_map/dot_general | solution.py:293
  55.2 0.0 reduce-scatter.2.cloned.1.call-update
  55.2 0.1 pad.2.clone
  55.3 0.9 slice.25
  56.2 0.8 slice.38
  57.0 0.8 slice.39
  57.8 0.8 slice.40
  58.5 1.3 collective-permute-start.1
  59.9 4.4 %convolution_convert_fusion.part = bf16[1024,2048]{1,0:T(8,128)(2,1)} fusion(bf16[1024,512]{1,0:T(8,128)(2,1)S(1)} %copy-done.7, bf16[512,2048]{1,0:T(8,128)(2,1)S(1)} %copy-done.4), kind=kOutput, calls=%fused_computation | convolution fusion | flops 2149580800 | bytes 7340032 | tf_op jit(solution)/shard_map/dot_general | solution.py:292
  64.3 2.8 %collective-permute-done.1.tail = bf16[192,512]{1,0:T(8,128)(2,1)S(1)} collective-permute-done((bf16[192,512]{1,0:T(8,128)(2,1)S(1)}, bf16[192,512]{1,0:T(8,128)(2,1)S(1)}, u32[]{:S(2)}, u32[]{:S(2)}) %collective-permute-start.1) | collective-permute-done | bytes 196640 | tf_op jit(solution)/shard_map/ppermute | solution.py:143
  67.1 0.7 copy-done.6
  67.8 26.9 %backward.1 = (bf16[3,1024,512]{2,1,0:T(8,128)(2,1)}, f32[3,7,512]{2,1,0:T(8,128)}) custom-call(bf16[1024,512]{1,0:T(8,128)(2,1)} %get-tuple-element.23.g, bf16[192,512]{1,0:T(8,128)(2,1)} %copy-done.6, f32[1024,512]{1,0:T(8,128)} %get-tuple-element.20.dq, f32[1024,512]{1,0:T(8,128)} %get-tuple-element.21.ks, f32[1024,512]{1,0:T(8,128)} %get-tuple-element.22.vs, ...), custom_call_target="tpu_custom_call" | custom-call | flops 10737418240 | bytes 20971520 | tf_op jit(solution)/shard_map/backward/pallas_call | solution.py:298
  94.7 0.8 reshape.16
  95.5 0.0 copy-done.2
  95.5 0.1 maximum_maximum_fusion.filt
  95.6 0.0 copy-start
  95.6 2.2 %copy-done = bf16[1024,2048]{1,0:T(8,128)(2,1)S(1)} copy-done((bf16[1024,2048]{1,0:T(8,128)(2,1)S(1)}, bf16[1024,2048]{1,0:T(8,128)(2,1)}, u32[]{:S(2)}) %copy-start) | copy-done | bytes 4194328
  97.9 57.5 %sums.1 = (bf16[1024,2048]{1,0:T(8,128)(2,1)S(1)}, f32[192,512]{1,0:T(8,128)S(1)}) custom-call(bf16[1024,2048]{1,0:T(8,128)(2,1)S(1)} %copy-done, f32[192,512]{1,0:T(8,128)S(1)} %maximum_maximum_fusion.filt), custom_call_target="tpu_custom_call" | custom-call | flops 12582912 | bytes 104857600 | tf_op jit(solution)/shard_map/sums/pallas_call | solution.py:218
  155.4 1.9 %copy-done.1 = bf16[1024,2048]{1,0:T(8,128)(2,1)} copy-done((bf16[1024,2048]{1,0:T(8,128)(2,1)}, bf16[1024,2048]{1,0:T(8,128)(2,1)S(1)}, u32[]{:S(2)}) %copy-start.1) | copy-done | bytes 4194328
  157.3 0.7 slice.29
  158.1 0.6 reshape.17
  158.7 1.9 %copy.14 = f32[256,512]{1,0:T(8,128)} copy(bf16[256,512]{0,1:T(8,128)(2,1)} %reduce-scatter.2.cloned.1.call-done) | data formatting | bytes 786432
  160.6 4.8 %copy.16 = bf16[1024,2048]{1,0:T(8,128)(2,1)} copy(bf16[1024,2048]{1,0:T(8,128)(2,1)} %copy-done.1) | data formatting | bytes 8388608
  (11 shorter events, 0.0 us)
Async XLA Ops:
  7.2 151.5 %reduce-scatter.2.cloned.1.call-start = ((), (), s32[]{:S(2)}) async-start(), calls=%async_computation.1 | async-start | bytes 2359296 | tf_op jit(solution)/shard_map/reduce_scatter | solution.py:296
  8.3 13.8 %collective-permute-start = (bf16[3,136,512]{2,1,0:T(8,128)(2,1)S(1)}, bf16[3,136,512]{2,1,0:T(8,128)(2,1)S(1)}, u32[]{:S(2)}, u32[]{:S(2)}) collective-permute-start(bf16[3,136,512]{2,1,0:T(8,128)(2,1)S(1)} %slice.31), channel_id=1, source_target_pairs={{0,4},{4,8},{8,12},{12,16},{16,20},{20,24},{24,28},{1,5},{5,9},{9,... | collective-permute-start | bytes 1253384 | tf_op jit(solution)/shard_map/ppermute | solution.py:143
  22.0 0.8 copy-start.5
  22.8 27.2 %copy-start.3 = (bf16[1024,2048]{1,0:T(8,128)(2,1)S(1)}, bf16[1024,2048]{1,0:T(8,128)(2,1)}, u32[]{:S(2)}) copy-start(bf16[1024,2048]{1,0:T(8,128)(2,1)} %og.1) | copy-start | bytes 12582916
  50.0 9.8 %copy-start.4 = (bf16[512,2048]{1,0:T(8,128)(2,1)S(1)}, bf16[512,2048]{1,0:T(8,128)(2,1)}, u32[]{:S(2)}) copy-start(bf16[512,2048]{1,0:T(8,128)(2,1)} %w.1) | copy-start | bytes 6291460
  50.0 9.8 %copy-start.7 = (bf16[1024,512]{1,0:T(8,128)(2,1)S(1)}, bf16[1024,512]{1,0:T(8,128)(2,1)}, u32[]{:S(2)}) copy-start(bf16[1024,512]{1,0:T(8,128)(2,1)} %get-tuple-element.17) | copy-start | bytes 3145732
  58.5 8.6 %collective-permute-start.1 = (bf16[192,512]{1,0:T(8,128)(2,1)S(1)}, bf16[192,512]{1,0:T(8,128)(2,1)S(1)}, u32[]{:S(2)}, u32[]{:S(2)}) collective-permute-start(bf16[192,512]{1,0:T(8,128)(2,1)S(1)} %pad_maximum_fusion), channel_id=1, source_target_pairs={{4,0},{8,4},{12,8},{16,12},{20,16},{24,20},{28,24},{5,1},{9,5},{13... | collective-permute-start | bytes 589832 | tf_op jit(solution)/shard_map/ppermute | solution.py:143
  64.3 31.3 %copy-start.2 = (f32[128,512]{1,0:T(8,128)S(1)}, f32[128,512]{1,0:T(8,128)}, u32[]{:S(2)}) copy-start(f32[128,512]{1,0:T(8,128)} %get-tuple-element.18) | copy-start | bytes 786436
  67.1 0.7 copy-start.6
  95.6 2.2 %copy-start = (bf16[1024,2048]{1,0:T(8,128)(2,1)S(1)}, bf16[1024,2048]{1,0:T(8,128)(2,1)}, u32[]{:S(2)}) copy-start(bf16[1024,2048]{1,0:T(8,128)(2,1)} %convolution_convert_fusion.part) | copy-start | bytes 12582916
  155.4 1.9 %copy-start.1 = (bf16[1024,2048]{1,0:T(8,128)(2,1)}, bf16[1024,2048]{1,0:T(8,128)(2,1)S(1)}, u32[]{:S(2)}) copy-start(bf16[1024,2048]{1,0:T(8,128)(2,1)S(1)} %get-tuple-element.39) | copy-start | bytes 12582916
Sparse Core Ops, SparseCore 0:
  55.3 75.4 reduce-scatter.1

commit v3 on v2

--- a/solution.py
+++ b/solution.py
@@ -143,22 +143,21 @@
     return lax.ppermute(value, axis, [(source, source + steps) for source in range(leading, last)])
 
 
-def sum_kernel(count, chunks, part, filt, out, total, near, mine, far, slots, sems, fsems):
+def sum_kernel(count, chunks, mine, far, filt, out, total, slots, sems, fsems):
     mesh_id = pl.DeviceIdType.MESH
     place = lax.axis_index("context")
     member = lax.axis_index("tensor")
     core = lax.rem(member, 2)
     sibling = (place, member + 1 - 2 * core)
-    peer = (place, lax.rem(member + 2, 4))
     others = [lax.rem(place + d, count) for d in range(1, count)]
-    half = part.shape[0] // 2
+    half = mine.shape[0]
     size = half // chunks
     piece = filt.shape[0] // count
 
     barrier = pltpu.get_barrier_semaphore()
-    for device in [sibling, peer] + [(other, member) for other in others]:
+    for device in [sibling] + [(other, member) for other in others]:
         pl.semaphore_signal(barrier, inc=1, device_id=device, device_id_type=mesh_id)
-    pl.semaphore_wait(barrier, count + 1)
+    pl.semaphore_wait(barrier, count)
 
     def send(source, target, pair, index, device):
         copy = pltpu.make_async_remote_copy(
@@ -174,17 +173,13 @@
     def rows_of(index):
         return pl.ds(pl.multiple_of(index * piece, piece), piece)
 
-    first = [
-        send(part.at[own_rows(1 - core, c)], near.at[c], sems, c, sibling) for c in range(chunks)
-    ]
     gather = [
         send(filt.at[rows_of(other)], slots.at[d], fsems, d, (other, member)) for d, other in enumerate(others)
     ]
-    second = []
+    third = []
     for c in range(chunks):
-        first[c].wait_recv()
-        mine[c] = (part[own_rows(core, c), :].astype(F32) + near[c].astype(F32)).astype(BF)
-        second.append(send(mine.at[c], far.at[c], sems, chunks + c, peer))
+        out[own_rows(core, c), :] = (mine[pl.ds(c * size, size), :].astype(F32) + far[pl.ds(c * size, size), :].astype(F32)).astype(BF)
+        third.append(send(out.at[own_rows(core, c)], out.at[own_rows(core, c)], sems, c, sibling))
     for copy in gather:
         copy.wait_recv()
     value = filt[rows_of(place), :]
@@ -195,25 +190,19 @@
         send(total.at[rows_of(place)], total.at[rows_of(place)], fsems, count - 1 + d, (other, member))
         for d, other in enumerate(others)
     ]
-    third = []
-    for c in range(chunks):
-        second[c].wait_recv()
-        out[own_rows(core, c), :] = (mine[c].astype(F32) + far[c].astype(F32)).astype(BF)
-        third.append(send(out.at[own_rows(core, c)], out.at[own_rows(core, c)], sems, 2 * chunks + c, sibling))
     for copy in spread + third:
         copy.wait_recv()
-    for copy in first + gather + second + spread + third:
+    for copy in gather + spread + third:
         copy.wait_send()
 
 
-def summed(partial_value, filters):
-    rows, feats = partial_value.shape
+def summed(mine, far, filters):
+    rows, feats = 2 * mine.shape[0], mine.shape[1]
     count = lax.axis_size("context")
     length, chans = filters.shape
     piece = -(-length // (8 * count)) * 8
     filters = jnp.concatenate([filters, jnp.zeros((piece * count - length, chans), F32)], axis=0)
     chunks = 4
-    size = rows // 2 // chunks
     vmem = pl.BlockSpec(memory_space=pltpu.VMEM)
     return pl.pallas_call(
         functools.partial(sum_kernel, count, chunks),
@@ -221,11 +210,11 @@
             jax.ShapeDtypeStruct((rows, feats), BF),
             jax.ShapeDtypeStruct((piece * count, chans), F32),
         ],
-        in_specs=[vmem, vmem],
+        in_specs=[vmem] * 3,
         out_specs=[vmem, vmem],
-        scratch_shapes=[pltpu.VMEM((chunks, size, feats), BF)] * 3 + [
+        scratch_shapes=[
             pltpu.VMEM((count - 1, piece, chans), F32),
-            pltpu.SemaphoreType.DMA((2, 3 * chunks)),
+            pltpu.SemaphoreType.DMA((2, chunks)),
             pltpu.SemaphoreType.DMA((2, 2 * (count - 1))),
         ],
         compiler_params=pltpu.CompilerParams(
@@ -233,7 +222,7 @@
         ),
         cost_estimate=pl.CostEstimate(flops=6 * rows * feats, bytes_accessed=100 * 2**20, transcendentals=0),
         name="sums",
-    )(partial_value, filters)
+    )(mine, far, filters)
 
 
 def shards(qkv, short_filter, long_filter, out_weight, out_grad):
@@ -294,7 +283,17 @@
         out_grad, mixed, (((0,), (0,)), ((), ())), preferred_element_type=F32
     ).astype(BF)
     weight_grad = lax.psum_scatter(weight_local, "context", scatter_dimension=0, tiled=True).astype(F32)
-    g, tail, _ = lax.optimization_barrier((g, tail, weight_local))
+    core = lax.rem(lax.axis_index("tensor"), 2)
+    half = rows // 2
+    near = lax.ppermute(
+        lax.dynamic_slice_in_dim(partial_value, (1 - core) * half, half, 0),
+        "tensor", [(0, 1), (1, 0), (2, 3), (3, 2)],
+    )
+    own = lax.dynamic_slice_in_dim(partial_value, core * half, half, 0)
+    mine = (own.astype(F32) + near.astype(F32)).astype(BF)
+    mine, tail = lax.optimization_barrier((mine, tail))
+    far = lax.ppermute(mine, "tensor", [(0, 2), (2, 0), (1, 3), (3, 1)])
+    g, tail, _, _ = lax.optimization_barrier((g, tail, weight_local, mine))
     grad, short_local = pl.pallas_call(
         functools.partial(second_kernel, n, pad, s),
         grid=(chans // cb,),
@@ -320,7 +319,7 @@
         name="backward",
     )(g, tail, dq, ks, vs, streams, halo, short, long_filter, *matrices)
     filters = jnp.concatenate([long_local, short_local.reshape(3 * s, chans)], axis=0)
-    output, filters = summed(partial_value, filters)
+    output, filters = summed(mine, far, filters)
     long_grad = filters[:n]
     short_grad = jnp.transpose(filters[n:n + 3 * s].reshape(3, s, chans), (1, 0, 2))
     return output, jnp.transpose(grad, (1, 0, 2)), long_grad, short_grad, weight_grad

time: 173 us -> 165 us (0.954)
  Pallas kernels: 112 us -> 81.5 us
  waiting for transfers between devices: 11.7 us -> 29.4 us
  other arithmetic: 0.11 us -> 3.12 us
  matrix products: 9.55 us -> 7.37 us
    pallas_call x1, Pallas kernels: 57.5 us -> 27.3 us  [summed(): pl.pallas_call(functools.partial(sum_kernel, count, chunks), out_shape=[j...]
    ppermute x0 -> x2, waiting for transfers between devices: none -> 16.4 us  [the longest x1 16.4 us: shards(): far = lax.ppermute(mine, 'tensor', [(0, 2), (2, 0), (1, 3), (3, 1)])]
    convert_element_type x0 -> x1, other arithmetic: none -> 3.01 us  [shards(): mine = (own.astype(F32) + near.astype(F32)).astype(BF)]
  transfers between devices with their start and end apart: 3 -> 5, of which waited for: 2 -> 3; matrix products, arithmetic and copies ran while one was open for 6% -> 8% of each run, Pallas kernels for 49% -> 33%
where the time goes in v3:
time: 165 us; the launch traced here: 163 us
  Pallas kernels  81.5 us (49%)
  waiting for transfers between devices  29.4 us (18%)
  local copies, waits for them, and re-layouts  20 us (12%)
  between operations  14.2 us (9%)
  starting transfers between devices  7.8 us (5%)
  matrix products  7.37 us (4%)
  other arithmetic  3.12 us (2%)
    pallas_call x1, Pallas kernels, summed(): pl.pallas_call(functools.partial(sum_kernel, count, chunks), out_shape=[j...  27.3 us
    pallas_call x1, Pallas kernels, shards(): pl.pallas_call(functools.partial(first_kernel, n, pad, s), grid=(chans //...  27.2 us
    pallas_call x1, Pallas kernels, shards(): pl.pallas_call(functools.partial(second_kernel, n, pad, s), grid=(chans /...  27 us
    ppermute x1, waiting for transfers between devices, shards(): far = lax.ppermute(mine, 'tensor', [(0, 2), (2, 0), (1, 3), (3, 1)])  16.4 us
    unnamed x18, local copies, waits for them, and re-layouts  13.3 us
    ppermute x2, waiting for transfers between devices, shifted(): lax.ppermute(value, axis, [(source, source + steps) for source in range(l...  13 us
    ppermute x2, starting transfers between devices, shifted(): lax.ppermute(value, axis, [(source, source + steps) for source in range(l...  6.19 us
    dot_general x1, matrix products, shards(): lax.dot_general(out_grad, mixed, (((0,), (0,)), ((), ())), preferred_elem...  3.72 us
  transfers between devices with their start and end apart: 5, of which 3 were waited for; matrix products, arithmetic and copies ran while one was open for 8% of the time, Pallas kernels for 33%

profile of v3, /device:TPU:0, one launch (start us, length us, event | category | flops | bytes accessed | tf_op | source)
XLA Modules:
  0.0 163.4 jit_solution(8394834024801700304)
XLA Ops:
  7.2 0.0 reduce-scatter.2.cloned.1.call-start
  7.2 1.0 slice.31
  8.3 4.9 %collective-permute-start = (bf16[3,136,512]{2,1,0:T(8,128)(2,1)S(1)}, bf16[3,136,512]{2,1,0:T(8,128)(2,1)S(1)}, u32[]{:S(2)}, u32[]{:S(2)}) collective-permute-start(bf16[3,136,512]{2,1,0:T(8,128)(2,1)S(1)} %slice.31), channel_id=1, source_target_pairs={{0,4},{4,8},{8,12},{12,16},{16,20},{20,24},{24,28},{1,5},{5,9},{9,... | collective-permute-start | bytes 1253384 | tf_op jit(solution)/shard_map/ppermute | solution.py:143
  13.2 8.8 %collective-permute-done.halo = bf16[3,136,512]{2,1,0:T(8,128)(2,1)S(1)} collective-permute-done((bf16[3,136,512]{2,1,0:T(8,128)(2,1)S(1)}, bf16[3,136,512]{2,1,0:T(8,128)(2,1)S(1)}, u32[]{:S(2)}, u32[]{:S(2)}) %collective-permute-start) | collective-permute-done | bytes 417824 | tf_op jit(solution)/shard_map/ppermute | solution.py:143
  22.0 0.8 copy-done.5
  22.8 27.2 %forward.1 = (bf16[1024,512]{1,0:T(8,128)(2,1)}, bf16[1024,512]{1,0:T(8,128)(2,1)}, f32[1024,512]{1,0:T(8,128)}, f32[1024,512]{1,0:T(8,128)}, f32[1024,512]{1,0:T(8,128)}, /*index=5*/f32[128,512]{1,0:T(8,128)}) custom-call(bf16[1024,2048]{1,0:T(8,128)(2,1)} %og.1, bf16[512,2048]{1,0:T(8,128)(2,1)} %w.1, bf16[3,1024,512]{2,1,0:T(8,128)(2,1)} %bitcast.11, ...), custom_call_target="tpu_custom_call" | custom-call | flops 4831838208 | bytes 20971520 | tf_op jit(solution)/shard_map/forward/pallas_call | solution.py:250
  50.0 3.7 %convolution_convert_fusion = bf16[1024,2048]{1,0:T(8,128)(2,1)S(1)} fusion(bf16[1024,512]{1,0:T(8,128)(2,1)} %get-tuple-element.19, bf16[512,2048]{1,0:T(8,128)(2,1)S(1)} %copy-done.4), kind=kOutput, calls=%fused_computation.1 | convolution fusion | flops 2149580800 | bytes 7340032 | tf_op jit(solution)/shard_map/dot_general | solution.py:281
  53.7 2.0 %copy-done.1 = bf16[1024,2048]{1,0:T(8,128)(2,1)} copy-done((bf16[1024,2048]{1,0:T(8,128)(2,1)}, bf16[1024,2048]{1,0:T(8,128)(2,1)S(1)}, u32[]{:S(2)}) %copy-start.1) | copy-done | bytes 4194328
  55.7 0.2 constant_dynamic-slice_fusion
  56.0 0.1 collective-permute-start.1
  56.0 1.9 %copy-done.3 = bf16[1024,2048]{1,0:T(8,128)(2,1)S(1)} copy-done((bf16[1024,2048]{1,0:T(8,128)(2,1)S(1)}, bf16[1024,2048]{1,0:T(8,128)(2,1)}, u32[]{:S(2)}) %copy-start.3) | copy-done | bytes 4194328
  57.9 3.7 %fusion = bf16[2048,512]{0,1:T(8,128)(2,1)} fusion(bf16[1024,512]{1,0:T(8,128)(2,1)S(1)} %copy-done.7, bf16[1024,2048]{1,0:T(8,128)(2,1)S(1)} %copy-done.3), kind=kOutput, calls=%fused_computation.3 | convolution fusion | flops 2148532224 | bytes 7340032 | tf_op jit(solution)/shard_map/dot_general | solution.py:282
  61.6 0.0 reduce-scatter.2.cloned.1.call-update
  61.6 0.9 slice.25
  62.6 0.8 slice.38
  63.3 0.8 slice.39
  64.1 0.8 slice.40
  64.9 1.3 collective-permute-start.2
  66.2 3.0 %add_convert_fusion.mine = bf16[512,2048]{1,0:T(8,128)(2,1)S(1)} fusion(bf16[512,2048]{1,0:T(8,128)(2,1)} %collective-permute-done.1, bf16[1024,2048]{1,0:T(8,128)(2,1)} %copy-done.1, s32[]{:T(128)S(6)} %select_n.6), kind=kLoop, calls=%fused_computation | loop fusion | flops 4194304 | bytes 6291460 | tf_op jit(solution)/shard_map/convert_element_type | solution.py:293
  69.2 4.2 %collective-permute-done.2.tail = bf16[192,512]{1,0:T(8,128)(2,1)S(1)} collective-permute-done((bf16[192,512]{1,0:T(8,128)(2,1)S(1)}, bf16[192,512]{1,0:T(8,128)(2,1)S(1)}, u32[]{:S(2)}, u32[]{:S(2)}) %collective-permute-start.2) | collective-permute-done | bytes 196640 | tf_op jit(solution)/shard_map/ppermute | solution.py:143
  73.4 1.5 collective-permute-start.3
  74.9 0.1 pad.2.clone
  75.0 27.0 %backward.1 = (bf16[3,1024,512]{2,1,0:T(8,128)(2,1)}, f32[3,7,512]{2,1,0:T(8,128)}) custom-call(bf16[1024,512]{1,0:T(8,128)(2,1)} %get-tuple-element.27.g, bf16[192,512]{1,0:T(8,128)(2,1)} %copy-done.6, f32[1024,512]{1,0:T(8,128)} %get-tuple-element.21.dq, f32[1024,512]{1,0:T(8,128)} %get-tuple-element.22.ks, f32[1024,512]{1,0:T(8,128)} %get-tuple-element.23.vs, ...), custom_call_target="tpu_custom_call" | custom-call | flops 10737418240 | bytes 20971520 | tf_op jit(solution)/shard_map/backward/pallas_call | solution.py:297
  102.0 0.8 reshape.16
  102.8 0.1 maximum_maximum_fusion.filt
  102.9 16.4 %collective-permute-done.3.far = bf16[512,2048]{1,0:T(8,128)(2,1)} collective-permute-done((bf16[512,2048]{1,0:T(8,128)(2,1)S(1)}, bf16[512,2048]{1,0:T(8,128)(2,1)}, u32[]{:S(2)}, u32[]{:S(2)}) %collective-permute-start.3) | collective-permute-done | bytes 2097184 | tf_op jit(solution)/shard_map/ppermute | solution.py:295
  119.3 27.3 %sums.1 = (bf16[1024,2048]{1,0:T(8,128)(2,1)S(1)}, f32[192,512]{1,0:T(8,128)S(1)}) custom-call(bf16[512,2048]{1,0:T(8,128)(2,1)S(1)} %add_convert_fusion.mine, bf16[512,2048]{1,0:T(8,128)(2,1)} %collective-permute-done.3.far, f32[192,512]{1,0:T(8,128)S(1)} %maximum_maximum_fusion.filt), custom_call_target="tpu_custom_call" | custom-call | flops 12582912 | bytes 104857600 | tf_op jit(solution)/shard_map/sums/pallas_call | solution.py:207
  146.6 1.9 %copy-done = bf16[1024,2048]{1,0:T(8,128)(2,1)} copy-done((bf16[1024,2048]{1,0:T(8,128)(2,1)}, bf16[1024,2048]{1,0:T(8,128)(2,1)S(1)}, u32[]{:S(2)}) %copy-start) | copy-done | bytes 4194328
  148.5 0.7 slice.29
  149.2 0.6 reshape.17
  149.9 1.9 %copy.14 = f32[256,512]{1,0:T(8,128)} copy(bf16[256,512]{0,1:T(8,128)(2,1)} %reduce-scatter.2.cloned.1.call-done) | data formatting | bytes 786432
  151.8 4.8 %copy.16 = bf16[1024,2048]{1,0:T(8,128)(2,1)} copy(bf16[1024,2048]{1,0:T(8,128)(2,1)} %copy-done) | data formatting | bytes 8388608
  (17 shorter events, 0.1 us)
Async XLA Ops:
  7.2 142.7 %reduce-scatter.2.cloned.1.call-start = ((), (), s32[]{:S(2)}) async-start(), calls=%async_computation.1 | async-start | bytes 2359296 | tf_op jit(solution)/shard_map/reduce_scatter | solution.py:285
  8.3 13.8 %collective-permute-start = (bf16[3,136,512]{2,1,0:T(8,128)(2,1)S(1)}, bf16[3,136,512]{2,1,0:T(8,128)(2,1)S(1)}, u32[]{:S(2)}, u32[]{:S(2)}) collective-permute-start(bf16[3,136,512]{2,1,0:T(8,128)(2,1)S(1)} %slice.31), channel_id=1, source_target_pairs={{0,4},{4,8},{8,12},{12,16},{16,20},{20,24},{24,28},{1,5},{5,9},{9,... | collective-permute-start | bytes 1253384 | tf_op jit(solution)/shard_map/ppermute | solution.py:143
  22.0 0.8 copy-start.5
  22.8 27.2 %copy-start.4 = (bf16[512,2048]{1,0:T(8,128)(2,1)S(1)}, bf16[512,2048]{1,0:T(8,128)(2,1)}, u32[]{:S(2)}) copy-start(bf16[512,2048]{1,0:T(8,128)(2,1)} %w.1) | copy-start | bytes 6291460
  50.0 6.0 %copy-start.7 = (bf16[1024,512]{1,0:T(8,128)(2,1)S(1)}, bf16[1024,512]{1,0:T(8,128)(2,1)}, u32[]{:S(2)}) copy-start(bf16[1024,512]{1,0:T(8,128)(2,1)} %get-tuple-element.19) | copy-start | bytes 3145732
  53.7 2.0 %copy-start.1 = (bf16[1024,2048]{1,0:T(8,128)(2,1)}, bf16[1024,2048]{1,0:T(8,128)(2,1)S(1)}, u32[]{:S(2)}) copy-start(bf16[1024,2048]{1,0:T(8,128)(2,1)S(1)} %convolution_convert_fusion) | copy-start | bytes 12582916
  55.7 2.2 %copy-start.3 = (bf16[1024,2048]{1,0:T(8,128)(2,1)S(1)}, bf16[1024,2048]{1,0:T(8,128)(2,1)}, u32[]{:S(2)}) copy-start(bf16[1024,2048]{1,0:T(8,128)(2,1)} %og.1) | copy-start | bytes 12582916
  56.0 10.2 %collective-permute-start.1 = (bf16[512,2048]{1,0:T(8,128)(2,1)S(1)}, bf16[512,2048]{1,0:T(8,128)(2,1)}, u32[]{:S(2)}, u32[]{:S(2)}) collective-permute-start(bf16[512,2048]{1,0:T(8,128)(2,1)S(1)} %constant_dynamic-slice_fusion), channel_id=1, source_target_pairs={{0,1},{1,0},{2,3},{3,2},{4,5},{5,4},{6,7},{7,6},{8,9},{9,8},{10,11... | collective-permute-start | bytes 6291464 | tf_op jit(solution)/shard_map/ppermute | solution.py:288
  64.9 8.5 %collective-permute-start.2 = (bf16[192,512]{1,0:T(8,128)(2,1)S(1)}, bf16[192,512]{1,0:T(8,128)(2,1)S(1)}, u32[]{:S(2)}, u32[]{:S(2)}) collective-permute-start(bf16[192,512]{1,0:T(8,128)(2,1)S(1)} %pad_maximum_fusion), channel_id=1, source_target_pairs={{4,0},{8,4},{12,8},{16,12},{20,16},{24,20},{28,24},{5,1},{9,5},{13... | collective-permute-start | bytes 589832 | tf_op jit(solution)/shard_map/ppermute | solution.py:143
  73.4 1.6 copy-start.6
  73.4 45.9 %collective-permute-start.3 = (bf16[512,2048]{1,0:T(8,128)(2,1)S(1)}, bf16[512,2048]{1,0:T(8,128)(2,1)}, u32[]{:S(2)}, u32[]{:S(2)}) collective-permute-start(bf16[512,2048]{1,0:T(8,128)(2,1)S(1)} %add_convert_fusion.mine), channel_id=1, source_target_pairs={{0,2},{2,0},{1,3},{3,1},{4,6},{6,4},{5,7},{7,5},{8,10},{10,8},{9,1... | collective-permute-start | bytes 6291464 | tf_op jit(solution)/shard_map/ppermute | solution.py:295
  75.0 27.8 %copy-start.2 = (f32[128,512]{1,0:T(8,128)S(1)}, f32[128,512]{1,0:T(8,128)}, u32[]{:S(2)}) copy-start(f32[128,512]{1,0:T(8,128)} %get-tuple-element.25) | copy-start | bytes 786436
  146.6 2.0 %copy-start = (bf16[1024,2048]{1,0:T(8,128)(2,1)}, bf16[1024,2048]{1,0:T(8,128)(2,1)S(1)}, u32[]{:S(2)}) copy-start(bf16[1024,2048]{1,0:T(8,128)(2,1)S(1)} %get-tuple-element.43) | copy-start | bytes 12582916
Sparse Core Ops, SparseCore 0:
  61.8 76.4 reduce-scatter.1
